TPU v7x, 32 devices: a whole 2x2x4 slice. The times are simulated.
32 devices in a mesh: groups: 2 (over y), px: 8 (over z, x), py: 2 (over core).
Axes of the slice: x: 2, y: 2, z: 4, core: 2. Of those that a mesh axis runs over, the one named last changes fastest.
Arguments:
- node_feat: bfloat16 [65536, 128], P(('groups', 'px', 'py')), parts along dimension 0, may hold values from -6 to 6
- edge_feat: bfloat16 [196608, 128], P(('groups', 'px', 'py')), parts along dimension 0, may hold values from -6 to 6
- edge_send: int32 [196608], P(('groups', 'px', 'py')), parts along dimension 0, may hold values from 0 to 2303, as said below
- edge_recv: int32 [196608], P(('groups', 'px', 'py')), parts along dimension 0, may hold values from 0 to 2048, as said below
- halo_send: int32 [64, 128], P(('groups', 'px', 'py')), parts along dimension 0, may hold values from 0 to 2048, as said below
- pool_slot: int32 [65536], P(('groups', 'px', 'py')), parts along dimension 0, may hold values from 0 to 127, as said below
- pool_node: int32 [32, 128], P(('groups', 'px', 'py')), parts along dimension 0, may hold values from 0 to 256, as said below
- coarse_send: int32 [24576], P(('groups', 'px', 'py')), parts along dimension 0, may hold values from 0 to 256, as said below
- coarse_recv: int32 [24576], P(('groups', 'px', 'py')), parts along dimension 0, may hold values from 0 to 256, as said below
- interp_pick: int32 [32, 128], P(('groups', 'px', 'py')), parts along dimension 0, may hold values from 0 to 256, as said below
- interp_slot: int32 [3, 65536], P(None, ('groups', 'px', 'py')), parts along dimension 1, may hold values from 0 to 127, as said below
- interp_wt: float32 [3, 65536], P(None, ('groups', 'px', 'py')), parts along dimension 1, as said below
- edge_in_w: bfloat16 [2, 384, 128], replicated, may hold values from -0.3125 to 0.3125
- pair_in_w: bfloat16 [4, 256, 128], replicated, may hold values from -0.375 to 0.375
- out_w: bfloat16 [6, 128, 128], replicated, may hold values from -0.5 to 0.5
- mlp_vec: float32 [6, 4, 128], replicated
Outputs:
- node_out: bfloat16 [65536, 128], P(('groups', 'px', 'py')), parts along dimension 0
There are 2 independent parts, one for each index of `groups`. A program takes and returns all parts, laid end to end along the dimension named above; an argument that names none is the same for every part. Nothing has to cross between parts.
Inputs may be any that keep to these rules, and one draw needn't show every extreme that they name: `edge_send`: values index a patch's extended table of 2304 rows. On every patch, rows below 5888 name only the patch's own nodes (128 to 2175), and their last 1 to 127 rows are padding with sender 128; the last 256 rows name live rim rows only: lower rim slots below the count the lower neighbour sends, upper rim slots likewise. `edge_recv`: padding rows of a patch's edges have receiver 2048; all others name a node of the patch. `halo_send`: each row holds a ragged count of live rows, then 2048 in the empty slots; counts lie between 64 and 128, and some patch sends a full 128 to a neighbour. Patch 0 sends nothing downward and the last patch nothing upward. `pool_slot`: the slot of a fine node is o * 8 + k with o a patch and k below that patch's number of slots for o (at most 8; some owner gets all 8 slots from every patch). `pool_node`: on patch o, entry p * 8 + k names a coarse node below 256 for the k that patch p uses toward o, and 256 for the others. `coarse_send`: on every patch the last 1 to 127 rows are padding with 256, the others name coarse nodes of that patch. `coarse_recv`: same rows of padding as coarse_send. `interp_pick`: on patch o, entry p * 8 + k names a coarse node for the k below the number of slots that patch p uses from o (at most 8; some owner fills all 8 for every patch), 256 elsewhere. `interp_slot`: each parent's slot is o * 8 + k with o a patch and k below the number of slots that the node's patch uses from o. `interp_wt`: Positive; the three weights of a node sum to one.
All inputs are finite; a program needn't handle non-finite values.
Results may differ from a plain program's by a relative error of at most 0.009.
Values may be sent and summed in bfloat16 or wider, within the bound.
A program may use at most 64 MiB of HBM per device.

v0:
```python
import jax
import jax.numpy as jnp
from jax import lax
from jax.sharding import PartitionSpec as P

NC = 256
PC = 8
QC = 8


def extended_2(value, sides, width):
    for axis, dim in sides:
        peers, length = (lax.axis_size(axis), value.shape[dim])
        up = [(i, (i + 1) % peers) for i in range(peers - 1)]
        down = [(j, i) for i, j in up]
        last = lax.slice_in_dim(value, length - width, length, axis=dim)
        first = lax.slice_in_dim(value, 0, width, axis=dim)
        before = lax.ppermute(last, axis, up)
        after = lax.ppermute(first, axis, down)
        value = jnp.concatenate([before, value, after], axis=dim)
    return value


def layer_norm(values, gain, shift):
    center = values - jnp.mean(values, axis=-1, keepdims=True)
    spread = jnp.mean(center * center, axis=-1, keepdims=True)
    return center * lax.rsqrt(spread + 1e-05) * gain + shift


def run_mlp(pieces, weight_in, weight_out, params):
    width = weight_out.shape[0]
    total = params[0]
    for place, piece in enumerate(pieces):
        total = total + jnp.dot(
            piece,
            weight_in[place * width : (place + 1) * width],
            preferred_element_type=jnp.float32,
        )
    hidden = jnp.maximum(total, 0.0).astype(jnp.bfloat16)
    result = jnp.dot(hidden, weight_out, preferred_element_type=jnp.float32) + params[1]
    return layer_norm(result, params[2], params[3])


def with_zero(table):
    return jnp.concatenate([table, jnp.zeros((1, table.shape[1]), table.dtype)], axis=0)


def summed(values, index, count):
    return jax.ops.segment_sum(values.astype(jnp.float32), index, num_segments=count + 1)[:count]


def rim_rows(nodes, rim_lists):
    outgoing = jnp.take(with_zero(nodes), rim_lists, axis=0)
    padded = extended_2(outgoing, ((("px", "py"), 0),), 1)
    return (padded[0], padded[3])


def edge_step(extended, nodes, edges, senders, receivers, weight_in, weight_out, params):
    source = jnp.take(extended, senders, axis=0)
    target = jnp.take(with_zero(nodes), receivers, axis=0)
    change = run_mlp([source, target, edges], weight_in, weight_out, params)
    return (edges.astype(jnp.float32) + change).astype(jnp.bfloat16)


def fine_layer(
    nodes, edges, senders, receivers, rim_lists, edge_in_w, pair_in_w, out_w, mlp_vec, layer
):
    weight_in = edge_in_w[layer]
    weight_out = out_w[2 * layer]
    params = mlp_vec[2 * layer]
    lower, upper = rim_rows(nodes, rim_lists)
    extended = jnp.concatenate([lower, nodes, upper], axis=0)
    updated = edge_step(extended, nodes, edges, senders, receivers, weight_in, weight_out, params)
    gathered = summed(updated, receivers, nodes.shape[0]).astype(jnp.bfloat16)
    node_change = run_mlp(
        [nodes, gathered], pair_in_w[layer], out_w[2 * layer + 1], mlp_vec[2 * layer + 1]
    )
    return ((nodes.astype(jnp.float32) + node_change).astype(jnp.bfloat16), updated)


def send_pooled(blocks):
    return lax.all_to_all(blocks, ("px", "py"), split_axis=0, concat_axis=0, tiled=True)


def send_coarse(blocks):
    return lax.all_to_all(blocks, ("px", "py"), split_axis=0, concat_axis=0, tiled=True)


def per_device(
    node_feat,
    edge_feat,
    edge_send,
    edge_recv,
    halo_send,
    pool_slot,
    pool_node,
    coarse_send,
    coarse_recv,
    interp_pick,
    interp_slot,
    interp_wt,
    edge_in_w,
    pair_in_w,
    out_w,
    mlp_vec,
):
    width = node_feat.shape[1]
    patches = lax.axis_size(("px", "py"))
    first_nodes, first_edges = fine_layer(
        node_feat,
        edge_feat,
        edge_send,
        edge_recv,
        halo_send,
        edge_in_w,
        pair_in_w,
        out_w,
        mlp_vec,
        0,
    )
    slots = (
        summed(first_nodes, pool_slot, patches * PC)
        .astype(jnp.bfloat16)
        .reshape(patches, PC, width)
    )
    arrived = send_pooled(slots).reshape(patches * PC, width)
    total = summed(arrived, pool_node[0], NC)
    center = total - jnp.mean(total, axis=-1, keepdims=True)
    spread = jnp.mean(center * center, axis=-1, keepdims=True)
    pooled = (center * lax.rsqrt(spread + 1e-05)).astype(jnp.bfloat16)
    table = with_zero(pooled)
    coarse_edges = run_mlp(
        [jnp.take(table, coarse_send, axis=0), jnp.take(table, coarse_recv, axis=0)],
        pair_in_w[2],
        out_w[4],
        mlp_vec[4],
    ).astype(jnp.bfloat16)
    coarse_agg = summed(coarse_edges, coarse_recv, NC).astype(jnp.bfloat16)
    coarse_nodes = (
        pooled.astype(jnp.float32)
        + run_mlp([pooled, coarse_agg], pair_in_w[3], out_w[5], mlp_vec[5])
    ).astype(jnp.bfloat16)
    outgoing = jnp.take(with_zero(coarse_nodes), interp_pick[0], axis=0).reshape(patches, QC, width)
    back = send_coarse(outgoing).reshape(patches * QC, width)
    rows = jnp.take(back, interp_slot, axis=0).astype(jnp.float32)
    mixed = (
        interp_wt[0][:, None] * rows[0]
        + interp_wt[1][:, None] * rows[1]
        + interp_wt[2][:, None] * rows[2]
    )
    second_nodes = (first_nodes.astype(jnp.float32) + mixed).astype(jnp.bfloat16)
    final_nodes, final_edges = fine_layer(
        second_nodes,
        first_edges,
        edge_send,
        edge_recv,
        halo_send,
        edge_in_w,
        pair_in_w,
        out_w,
        mlp_vec,
        1,
    )
    return final_nodes


def solution(mesh):
    placed = (
        P(("groups", "px", "py"), None),
        P(("groups", "px", "py"), None),
        P(("groups", "px", "py")),
        P(("groups", "px", "py")),
        P(("groups", "px", "py"), None),
        P(("groups", "px", "py")),
        P(("groups", "px", "py"), None),
        P(("groups", "px", "py")),
        P(("groups", "px", "py")),
        P(("groups", "px", "py"), None),
        P(None, ("groups", "px", "py")),
        P(None, ("groups", "px", "py")),
        P(),
        P(),
        P(),
        P(),
    )
    return jax.shard_map(
        per_device,
        mesh=mesh,
        in_specs=placed,
        out_specs=P(("groups", "px", "py"), None),
        check_vma=False,
    )
```

profile of v0, /device:TPU:0, one launch (start us, length us, event | category | flops | bytes accessed | tf_op | source)
XLA Modules:
  0.0 288.0 jit_solution(5895874014723853608)
XLA Ops:
  3.6 2.4 collective-permute-start
  15.4 22.1 %gather_fusion.4 = bf16[6144,128]{1,0:T(8,128)(2,1)} fusion(bf16[2049,128]{1,0:T(8,128)(2,1)S(1)} %concatenate.20, s32[6144]{0:T(1024)S(1)} %fusion.112), kind=kCustom, calls=%fused_computation.2.clone | custom fusion | bytes 3170304 | tf_op jit(solution)/shard_map/jit(_take)/gather | solution.py:60
  39.1 18.1 %gather_fusion.3 = bf16[6144,128]{1,0:T(8,128)(2,1)S(1)} fusion(bf16[2304,128]{1,0:T(8,128)(2,1)S(1)} %pad_maximum_fusion, s32[6144]{0:T(1024)S(1)} %fusion.111), kind=kCustom, calls=%fused_computation.1.clone | custom fusion | bytes 3170304 | tf_op jit(solution)/shard_map/jit(_take)/gather | solution.py:59
  59.1 5.6 %convolution_add_fusion.6 = f32[6144,128]{1,0:T(8,128)} fusion(f32[6144,128]{1,0:T(8,128)S(1)} %convolution_add_fusion.7, bf16[6144,128]{1,0:T(8,128)(2,1)S(1)} %copy-done.8, pred[6144]{0:T(1024)(128)(4,1)S(1)} %compare_and_fusion.1, bf16[2,384,128]{2,1,0:T(8,128)(2,1)} %param.36), kind=kOutput, calls=%fused_computation.23 | convolution fusion | flops 202899456 | bytes 7903232 | tf_op jit(solution)/shard_map/dot_general | solution.py:34
  64.7 3.5 %fusion.131 = (f32[6144]{0:T(1024)S(1)}, f32[6144,128]{0,1:T(8,128)S(1)}) fusion(f32[128]{0:T(128)} %get-tuple-element.37, bf16[6,128,128]{2,1,0:T(8,128)(2,1)} %param.38, f32[6144,128]{1,0:T(8,128)} %convolution_add_fusion.6, bf16[6144,128]{1,0:T(8,128)(2,1)} %param.25, bf16[2,384,128]{2,1,0:T(8,128)(2,1)} %param.36), kind=kOutput, calls=%fused_computation.238 | convolution fusion | flops 406579200 | bytes 7954944 | tf_op jit(solution)/shard_map/dot_general | solution.py:40
  71.6 3.1 %copy.20 = f32[6144,128]{1,0:T(8,128)} copy(bf16[6144,128]{0,1:T(8,128)(2,1)} %add_convert_fusion.1) | data formatting | bytes 4718592 | tf_op jit(solution)/shard_map/convert_element_type | solution.py:49
  74.6 33.9 %scatter_custom_fusion = f32[2049,128]{1,0:T(8,128)S(1)} fusion(s32[6144]{0:T(1024)S(1)} %copy-done.13, f32[6144,128]{1,0:T(8,128)} %copy.20, f32[]{:T(128)} %constant.66.clone.1), kind=kCustom, calls=%fused_computation.87 | custom fusion | flops 786432 | bytes 1049600 | tf_op jit(solution)/shard_map/scatter-add | solution.py:49
  108.6 1.9 fusion.134
  111.9 11.6 %scatter_custom_fusion.1 = f32[129,128]{1,0:T(8,128)S(1)} fusion(s32[2048]{0:T(1024)} %param.29, bf16[2048,128]{1,0:T(8,128)(2,1)S(1)} %add_convert_fusion.3, f32[]{:T(128)} %constant.66.clone.1), kind=kCustom, calls=%fused_computation.52 | custom fusion | flops 524288 | bytes 590848 | tf_op jit(solution)/shard_map/scatter-add | solution.py:49
  124.2 9.2 %all-to-all-start = ((bf16[16,8,128]{2,1,0:T(8,128)(2,1)}), bf16[16,8,128]{2,1,0:T(8,128)(2,1)S(1)}, u32[]{:S(2)}, u32[]{:S(2)}) async-start(bf16[16,8,128]{2,1,0:T(8,128)(2,1)} %fusion.57), calls=%async_computation | async-start | bytes 65536 | tf_op jit(solution)/shard_map/all_to_all | solution.py:82
  133.4 6.6 %all-to-all-done = bf16[16,8,128]{2,1,0:T(8,128)(2,1)S(1)} async-done(((bf16[16,8,128]{2,1,0:T(8,128)(2,1)}), bf16[16,8,128]{2,1,0:T(8,128)(2,1)S(1)}, u32[]{:S(2)}, u32[]{:S(2)}) %all-to-all-start) | async-done | bytes 32800 | tf_op jit(solution)/shard_map/all_to_all | solution.py:82
  146.8 6.2 %scatter_custom_fusion.3 = f32[257,128]{1,0:T(8,128)S(1)} fusion(s32[768]{0:T(1024)} %param.32, f32[768,128]{1,0:T(8,128)S(1)} %copy.21, f32[]{:T(128)} %constant.66.clone.1), kind=kCustom, calls=%fused_computation.111 | custom fusion | flops 98304 | bytes 132096 | tf_op jit(solution)/shard_map/scatter-add | solution.py:49
  155.4 3.5 %all-to-all-start.1 = ((bf16[16,8,128]{2,1,0:T(8,128)(2,1)}), bf16[16,8,128]{2,1,0:T(8,128)(2,1)S(1)}, u32[]{:S(2)}, u32[]{:S(2)}) async-start(bf16[16,8,128]{2,1,0:T(8,128)(2,1)} %bitcast_select_fusion), calls=%async_computation.1 | async-start | bytes 65536 | tf_op jit(solution)/shard_map/all_to_all | solution.py:86
  158.9 6.6 %all-to-all-done.1 = bf16[16,8,128]{2,1,0:T(8,128)(2,1)S(1)} async-done(((bf16[16,8,128]{2,1,0:T(8,128)(2,1)}), bf16[16,8,128]{2,1,0:T(8,128)(2,1)S(1)}, u32[]{:S(2)}, u32[]{:S(2)}) %all-to-all-start.1) | async-done | bytes 32800 | tf_op jit(solution)/shard_map/all_to_all | solution.py:86
  165.5 18.1 %gather_fusion.1 = bf16[6144,128]{1,0:T(8,128)(2,1)S(1)} fusion(bf16[128,128]{1,0:T(8,128)(2,1)S(1)} %bitcast.194, s32[6144]{0:T(1024)S(1)} %broadcast_clamp_fusion), kind=kCustom, calls=%fused_computation.9 | custom fusion | bytes 3170304 | tf_op jit(solution)/shard_map/jit(_take)/gather | solution.py:145
  191.3 22.1 %gather_fusion.9 = bf16[6144,128]{1,0:T(8,128)(2,1)} fusion(bf16[2049,128]{1,0:T(8,128)(2,1)S(1)} %concatenate.24, s32[6144]{0:T(1024)S(1)} %fusion.112), kind=kCustom, calls=%fused_computation.6.clone | custom fusion | bytes 3170304 | tf_op jit(solution)/shard_map/jit(_take)/gather | solution.py:60
  213.5 18.1 %gather_fusion.8 = bf16[6144,128]{1,0:T(8,128)(2,1)S(1)} fusion(bf16[2304,128]{1,0:T(8,128)(2,1)S(1)} %pad_maximum_fusion.1, s32[6144]{0:T(1024)S(1)} %fusion.111), kind=kCustom, calls=%fused_computation.5.clone | custom fusion | bytes 3170304 | tf_op jit(solution)/shard_map/jit(_take)/gather | solution.py:59
  231.6 1.9 convolution_add_fusion.3
  233.5 5.6 %convolution_add_fusion.2 = f32[6144,128]{1,0:T(8,128)} fusion(f32[6144,128]{1,0:T(8,128)S(1)} %convolution_add_fusion.3, bf16[6144,128]{1,0:T(8,128)(2,1)S(1)} %copy-done.7, pred[6144]{0:T(1024)(128)(4,1)S(1)} %compare_and_fusion.1, bf16[2,384,128]{2,1,0:T(8,128)(2,1)} %param.36), kind=kOutput, calls=%fused_computation.18 | convolution fusion | flops 202899456 | bytes 7903232 | tf_op jit(solution)/shard_map/dot_general | solution.py:34
  239.1 3.6 %fusion.145 = (f32[6144]{0:T(1024)S(1)}, f32[6144,128]{0,1:T(8,128)S(1)}) fusion(f32[128]{0:T(128)S(1)} %copy-done.31, bf16[6,128,128]{2,1,0:T(8,128)(2,1)} %param.38, f32[6144,128]{1,0:T(8,128)} %convolution_add_fusion.2, bf16[6144,128]{0,1:T(8,128)(2,1)} %add_convert_fusion.1, bf16[2,384,128]{2,1,0:T(8,128)(2,1)} %param.36), kind=kOutput, calls=%fused_computation.242 | convolution fusion | flops 406579200 | bytes 7954944 | tf_op jit(solution)/shard_map/dot_general | solution.py:40
  244.2 2.3 fusion.8
  246.5 3.6 %copy.22 = f32[6144,128]{1,0:T(8,128)} copy(f32[6144,128]{0,1:T(8,128)} %fusion.8) | data formatting | bytes 6291456 | tf_op jit(solution)/shard_map/convert_element_type | solution.py:49
  250.0 33.9 %scatter_custom_fusion.4 = f32[2049,128]{1,0:T(8,128)S(1)} fusion(s32[6144]{0:T(1024)S(1)} %copy-done.13, f32[6144,128]{1,0:T(8,128)} %copy.22, f32[]{:T(128)} %constant.66.clone.1), kind=kCustom, calls=%fused_computation.85 | custom fusion | flops 786432 | bytes 1049600 | tf_op jit(solution)/shard_map/scatter-add | solution.py:49
  283.9 1.9 fusion.148
  (194 shorter events, 41.7 us)
Async XLA Ops:
  0.0 13.5 %copy-start.3 = (bf16[2048,128]{1,0:T(8,128)(2,1)S(1)}, bf16[2048,128]{1,0:T(8,128)(2,1)}, u32[]{:S(2)}) copy-start(bf16[2048,128]{1,0:T(8,128)(2,1)} %param.24) | copy-start | bytes 1572868
  0.0 8.7 %copy-start.20 = (s32[768]{0:T(1024)S(1)}, s32[768]{0:T(1024)}, u32[]{:S(2)}) copy-start(s32[768]{0:T(1024)} %param.31) | copy-start | bytes 9220
  0.0 9.2 %copy-start.21 = (s32[768]{0:T(1024)S(1)}, s32[768]{0:T(1024)}, u32[]{:S(2)}) copy-start(s32[768]{0:T(1024)} %param.32) | copy-start | bytes 9220
  0.0 9.8 %copy-start.11 = (s32[3,2048]{1,0:T(4,128)S(1)}, s32[3,2048]{1,0:T(4,128)}, u32[]{:S(2)}) copy-start(s32[3,2048]{1,0:T(4,128)} %param.34) | copy-start | bytes 73732
  0.0 10.5 %copy-start.51 = (s32[1,128]{1,0:T(1,128)S(1)}, s32[1,128]{1,0:T(1,128)}, u32[]{:S(2)}) copy-start(s32[1,128]{1,0:T(1,128)} %param.33) | copy-start | bytes 1540
  0.0 12.8 %copy-start.17 = (f32[3,2048]{1,0:T(4,128)S(1)}, f32[3,2048]{1,0:T(4,128)}, u32[]{:S(2)}) copy-start(f32[3,2048]{1,0:T(4,128)} %param.35) | copy-start | bytes 73732
  0.1 13.4 %copy-start.9 = (bf16[4,256,128]{2,1,0:T(8,128)(2,1)S(1)}, bf16[4,256,128]{2,1,0:T(8,128)(2,1)}, u32[]{:S(2)}) copy-start(bf16[4,256,128]{2,1,0:T(8,128)(2,1)} %param.37) | copy-start | bytes 786436
  1.6 13.2 %copy-start.27 = (pred[2,128]{1,0:T(4,128)(4,1)}, pred[2,128]{1,0:T(4,128)(4,1)S(1)}, u32[]{:S(2)}) copy-start(pred[2,128]{1,0:T(4,128)(4,1)S(1)} %compare_and_fusion.6) | copy-start | bytes 772
  3.6 35.4 %collective-permute-start = (bf16[1,128,128]{2,1,0:T(8,128)(2,1)S(1)}, bf16[1,128,128]{2,1,0:T(8,128)(2,1)S(1)}, u32[]{:S(2)}, u32[]{:S(2)}) collective-permute-start(bf16[1,128,128]{2,1,0:T(8,128)(2,1)S(1)} %get-tuple-element.10), channel_id=1, source_target_pairs={{0,1},{1,2},{2,3},{3,4},{4,5},{5,6},{6,7},{7,8},{8,9},{9,10},{10,1... | collective-permute-start | bytes 98312 | tf_op jit(solution)/shard_map/ppermute | solution.py:18
  6.0 33.0 %collective-permute-start.1 = (bf16[1,128,128]{2,1,0:T(8,128)(2,1)S(1)}, bf16[1,128,128]{2,1,0:T(8,128)(2,1)S(1)}, u32[]{:S(2)}, u32[]{:S(2)}) collective-permute-start(bf16[1,128,128]{2,1,0:T(8,128)(2,1)S(1)} %get-tuple-element.12), channel_id=1, source_target_pairs={{1,0},{2,1},{3,2},{4,3},{5,4},{6,5},{7,6},{8,7},{9,8},{10,9},{11,1... | collective-permute-start | bytes 98312 | tf_op jit(solution)/shard_map/ppermute | solution.py:19
  15.4 22.1 %copy-start.5 = (bf16[6144,128]{1,0:T(8,128)(2,1)S(1)}, bf16[6144,128]{1,0:T(8,128)(2,1)}, u32[]{:S(2)}) copy-start(bf16[6144,128]{1,0:T(8,128)(2,1)} %param.25) | copy-start | bytes 4718596
  71.6 37.0 %copy-start.10 = (bf16[6,128,128]{2,1,0:T(8,128)(2,1)S(1)}, bf16[6,128,128]{2,1,0:T(8,128)(2,1)}, u32[]{:S(2)}) copy-start(bf16[6,128,128]{2,1,0:T(8,128)(2,1)} %param.38) | copy-start | bytes 589828
  71.6 37.0 %copy-start.46 = (f32[128]{0:T(128)S(1)}, f32[128]{0:T(128)}, u32[]{:S(2)}) copy-start(f32[128]{0:T(128)} %get-tuple-element.33) | copy-start | bytes 1540
  111.1 22.3 %copy-start.50 = (s32[128]{0:T(128)S(1)}, s32[128]{0:T(128)}, u32[]{:S(2)}) copy-start(s32[128]{0:T(128)} %fusion.113) | copy-start | bytes 1540
  111.2 30.5 %copy-start.18 = (s32[1024]{0:T(1024)S(1)}, s32[1024]{0:T(1024)}, u32[]{:S(2)}) copy-start(s32[1024]{0:T(1024)} %pad_clamp_fusion.2) | copy-start | bytes 12292
  111.9 31.7 %copy-start.19 = (s32[1024]{0:T(1024)S(1)}, s32[1024]{0:T(1024)}, u32[]{:S(2)}) copy-start(s32[1024]{0:T(1024)} %pad_clamp_fusion.1) | copy-start | bytes 12292
  124.2 15.8 %all-to-all-start = ((bf16[16,8,128]{2,1,0:T(8,128)(2,1)}), bf16[16,8,128]{2,1,0:T(8,128)(2,1)S(1)}, u32[]{:S(2)}, u32[]{:S(2)}) async-start(bf16[16,8,128]{2,1,0:T(8,128)(2,1)} %fusion.57), calls=%async_computation | async-start | bytes 65536 | tf_op jit(solution)/shard_map/all_to_all | solution.py:82
  146.5 8.2 %copy-start.24 = (pred[16,8]{1,0:T(8,128)(4,1)S(1)}, pred[16,8]{1,0:T(8,128)(4,1)}, u32[]{:S(2)}) copy-start(pred[16,8]{1,0:T(8,128)(4,1)} %compare_and_fusion.3) | copy-start | bytes 388
  155.4 10.1 %all-to-all-start.1 = ((bf16[16,8,128]{2,1,0:T(8,128)(2,1)}), bf16[16,8,128]{2,1,0:T(8,128)(2,1)S(1)}, u32[]{:S(2)}, u32[]{:S(2)}) async-start(bf16[16,8,128]{2,1,0:T(8,128)(2,1)} %bitcast_select_fusion), calls=%async_computation.1 | async-start | bytes 65536 | tf_op jit(solution)/shard_map/all_to_all | solution.py:86
  185.7 27.7 %copy-start.1 = (bf16[2048,128]{1,0:T(8,128)(2,1)}, bf16[2048,128]{1,0:T(8,128)(2,1)S(1)}, u32[]{:S(2)}) copy-start(bf16[2048,128]{1,0:T(8,128)(2,1)S(1)} %fusion.23) | copy-start | bytes 1572868
  186.9 26.5 %collective-permute-start.2 = (bf16[1,128,128]{2,1,0:T(8,128)(2,1)S(1)}, bf16[1,128,128]{2,1,0:T(8,128)(2,1)S(1)}, u32[]{:S(2)}, u32[]{:S(2)}) collective-permute-start(bf16[1,128,128]{2,1,0:T(8,128)(2,1)S(1)} %get-tuple-element.6), channel_id=1, source_target_pairs={{0,1},{1,2},{2,3},{3,4},{4,5},{5,6},{6,7},{7,8},{8,9},{9,10},{10,1... | collective-permute-start | bytes 98312 | tf_op jit(solution)/shard_map/ppermute | solution.py:18
  188.5 24.9 %collective-permute-start.3 = (bf16[1,128,128]{2,1,0:T(8,128)(2,1)S(1)}, bf16[1,128,128]{2,1,0:T(8,128)(2,1)S(1)}, u32[]{:S(2)}, u32[]{:S(2)}) collective-permute-start(bf16[1,128,128]{2,1,0:T(8,128)(2,1)S(1)} %get-tuple-element.8), channel_id=1, source_target_pairs={{1,0},{2,1},{3,2},{4,3},{5,4},{6,5},{7,6},{8,7},{9,8},{10,9},{11,1... | collective-permute-start | bytes 98312 | tf_op jit(solution)/shard_map/ppermute | solution.py:19
  213.5 18.1 %copy-start.47 = (f32[128]{0:T(128)S(1)}, f32[128]{0:T(128)}, u32[]{:S(2)}) copy-start(f32[128]{0:T(128)} %get-tuple-element.21) | copy-start | bytes 1540
  246.5 37.4 %copy-start.43 = (f32[128]{0:T(128)S(1)}, f32[128]{0:T(128)}, u32[]{:S(2)}) copy-start(f32[128]{0:T(128)} %get-tuple-element.17) | copy-start | bytes 1540
  (34 other events, 117.8 us)
where the time goes:
time: 290 us; the launch traced here: 288 us
  local copies, waits for them, and re-layouts  120 us (41%)
  other arithmetic  105 us (36%)
  matrix products  29.8 us (10%)
  starting transfers between devices  19.5 us (7%)
  waiting for transfers between devices  13.2 us (5%)
    scatter-add x5, other arithmetic, summed(): jax.ops.segment_sum(values.astype(jnp.float32), index, num_segments=count...  86.7 us
    gather x2, local copies, waits for them, and re-layouts, edge_step(): target = jnp.take(with_zero(nodes), receivers, axis=0)  44.1 us
    gather x2, local copies, waits for them, and re-layouts, edge_step(): source = jnp.take(extended, senders, axis=0)  36.2 us
    gather x1, local copies, waits for them, and re-layouts, per_device(): rows = jnp.take(back, interp_slot, axis=0).astype(jnp.float32)  18.1 us
    dot_general x8, matrix products, run_mlp(): jnp.dot(piece, weight_in[place * width:(place + 1) * width], preferred_el...  18 us
    dot_general x6, matrix products, run_mlp(): jnp.dot(hidden, weight_out, preferred_element_type=jnp.float32) + params[1]  11.8 us
    all_to_all x1, starting transfers between devices, send_pooled(): lax.all_to_all(blocks, ('px', 'py'), split_axis=0, concat_axis=0, tiled=T...  9.21 us
    convert_element_type x3, local copies, waits for them, and re-layouts, summed(): values.astype(jnp.float32)  6.78 us
  transfers between devices with their start and end apart: 6, of which 2 were waited for; matrix products, arithmetic and copies ran while one was open for 19% of the time, Pallas kernels for 0%

commit v1 on v0

v1 whole, which is shorter than its diff:
```python
import functools

import jax
import jax.numpy as jnp
from jax import lax
from jax.experimental import pallas as pl
from jax.experimental.pallas import tpu as pltpu
from jax.sharding import PartitionSpec as P

LANES = 128
NC = 256
SLOT = 8
RIM = 128
BLOCKS = 4
TILE = 1024
BF16 = jnp.bfloat16
F32 = jnp.float32


def dot(a, b):
    return jnp.dot(a, b, preferred_element_type=F32)


def column(row):
    return jnp.broadcast_to(row, (LANES, LANES)).T


def columns(ref, start, count):
    return jnp.concatenate([column(ref[pl.ds(start + i, 1), :]) for i in range(count)], axis=0)


def hot(mask):
    return jnp.where(mask, 1.0, 0.0).astype(BF16)


def hot_rows(col, width):
    lane = lax.broadcasted_iota(jnp.int32, col.shape, 1)
    return jnp.concatenate([hot(col == lane + k) for k in range(0, width, LANES)], axis=1)


def hot_columns(rows, height):
    place = lax.broadcasted_iota(jnp.int32, (height, LANES), 0)
    return jnp.concatenate([hot(place == row) for row in rows], axis=1)


def table_of(nodes_ref):
    part = nodes_ref.shape[0] // BLOCKS
    return jnp.concatenate([nodes_ref[b * part : (b + 1) * part, :] for b in range(BLOCKS)], axis=1)


def pick_rows(table, col):
    part = table.shape[0]
    shift = part.bit_length() - 1
    wide = dot(hot_rows(col & (part - 1), part), table)
    block = col >> shift
    out = jnp.zeros(col.shape, F32)
    for b in range(BLOCKS):
        out = jnp.where(block == b, wide[:, b * LANES : (b + 1) * LANES], out)
    return out.astype(BF16)


def normed(values):
    center = values - jnp.mean(values, axis=-1, keepdims=True)
    spread = jnp.mean(center * center, axis=-1, keepdims=True)
    return center * lax.rsqrt(spread + 1e-05)


def run_mlp(pieces, weights, out_w, vec, i):
    both = jnp.concatenate(pieces, axis=1)
    total = dot(both, weights) + vec[i, 0:1, :]
    hidden = jnp.maximum(total, 0.0).astype(BF16)
    result = dot(hidden, out_w[i]) + vec[i, 1:2, :]
    return normed(result) * vec[i, 2:3, :] + vec[i, 3:4, :]


def kernel(
    node,
    edge,
    send,
    recv,
    halo,
    pslot,
    pnode,
    csend,
    crecv,
    ipick,
    islot,
    iwt,
    edge_w,
    pair_w,
    out_w,
    vec,
    out,
    scol,
    rcol,
    e1,
    h1,
    h2,
    acc,
    rim_out,
    rims,
    slots,
    arrived,
    picks,
    back,
    rim_sem,
    pool_sem,
    back_sem,
):
    py = lax.axis_size("py")
    peers = lax.axis_size("px") * py
    me = lax.axis_index("px") * py + lax.axis_index("py")
    nf = node.shape[0]
    ef = edge.shape[0]
    part = nf // BLOCKS
    tiles = ef // TILE
    rows = TILE // LANES
    eb = 2 * RIM

    def place(q):
        return {"px": q // py, "py": lax.rem(q, py)}

    barrier = pltpu.get_barrier_semaphore()

    def greet(d, carry):
        pl.semaphore_signal(
            barrier,
            inc=1,
            device_id=place(lax.rem(me + d, peers)),
            device_id_type=pl.DeviceIdType.MESH,
        )
        return carry

    lax.fori_loop(1, peers, greet, 0)

    def rim_copy(layer, side):
        other = me + (1 if side else -1)
        return pltpu.make_async_remote_copy(
            src_ref=rim_out.at[layer, side],
            dst_ref=rims.at[layer, 1 - side],
            send_sem=rim_sem.at[0, layer, side],
            recv_sem=rim_sem.at[1, layer, 1 - side],
            device_id=place(jnp.clip(other, 0, peers - 1)),
            device_id_type=pl.DeviceIdType.MESH,
        )

    def send_rims(layer, table):
        for side in range(2):
            rim_out[layer, side] = pick_rows(table, column(halo[side : side + 1, :]))
        if layer == 0:
            pl.semaphore_wait(barrier, peers - 1)
        for side in range(2):
            edge_patch = 0 if side == 0 else peers - 1

            @pl.when(me != edge_patch)
            def _(side=side):
                rim_copy(layer, side).start()

            @pl.when(me == edge_patch)
            def _(side=side):
                rims[layer, side] = jnp.zeros((RIM, LANES), BF16)

    def wait_rims(layer):
        for side in range(2):
            edge_patch = 0 if side == 0 else peers - 1

            @pl.when(me != edge_patch)
            def _(side=side):
                copy = rim_copy(layer, side)
                copy.wait_send()
                pltpu.make_async_remote_copy(
                    src_ref=rim_out.at[layer, side],
                    dst_ref=rims.at[layer, side],
                    send_sem=rim_sem.at[0, layer, side],
                    recv_sem=rim_sem.at[1, layer, side],
                    device_id=place(jnp.clip(me + (1 if side else -1), 0, peers - 1)),
                    device_id_type=pl.DeviceIdType.MESH,
                ).wait_recv()

    def exchange(src, dst, sem, d):
        q = lax.rem(me + d, peers)
        return pltpu.make_async_remote_copy(
            src_ref=src.at[pl.ds(pl.multiple_of(q * SLOT, SLOT), SLOT), :],
            dst_ref=dst.at[pl.ds(pl.multiple_of(me * SLOT, SLOT), SLOT), :],
            send_sem=sem.at[0, d],
            recv_sem=sem.at[1, d],
            device_id=place(q),
            device_id_type=pl.DeviceIdType.MESH,
        )

    def arrival(src, dst, sem, d):
        q = lax.rem(me + peers - d, peers)
        return pltpu.make_async_remote_copy(
            src_ref=src.at[pl.ds(pl.multiple_of(q * SLOT, SLOT), SLOT), :],
            dst_ref=dst.at[pl.ds(pl.multiple_of(q * SLOT, SLOT), SLOT), :],
            send_sem=sem.at[0, d],
            recv_sem=sem.at[1, d],
            device_id=place(q),
            device_id_type=pl.DeviceIdType.MESH,
        )

    def all_to_all(src, dst, sem):
        def start(d, carry):
            exchange(src, dst, sem, d).start()
            return carry

        def finish(d, carry):
            exchange(src, dst, sem, d).wait_send()
            arrival(src, dst, sem, d).wait_recv()
            return carry

        lax.fori_loop(1, peers, start, 0)
        mine = pl.ds(pl.multiple_of(me * SLOT, SLOT), SLOT)
        dst[mine, :] = src[mine, :]
        lax.fori_loop(1, peers, finish, 0)

    def fine_layer(layer, nodes, edges, new_edges, new_nodes):
        table = table_of(nodes)
        send_rims(layer, table)
        acc[...] = jnp.zeros(acc.shape, F32)

        def edge_tile(t, last):
            at = pl.ds(pl.multiple_of(t * TILE, TILE), TILE)
            if layer == 0:
                to = columns(recv, t * rows, rows)
                of = columns(send, t * rows, rows)
                rcol[at, :] = to
                scol[at, :] = of
            else:
                to = rcol[at, :]
                of = scol[at, :]
            tab = table_of(nodes)
            source = pick_rows(tab, of - RIM)
            if last:
                tail = of[TILE - eb :]
                rim_row = jnp.where(tail < RIM, tail, tail - nf)
                rim = jnp.concatenate([rims[layer, 0], rims[layer, 1]], axis=0)
                more = dot(hot_rows(rim_row, eb), rim).astype(BF16)
                source = jnp.concatenate([source[: TILE - eb], more], axis=0)
            target = pick_rows(tab, to)
            old = edges[at, :]
            change = run_mlp([source, target, old], edge_w[layer], out_w, vec, 2 * layer)
            new = (old.astype(F32) + change).astype(BF16)
            if new_edges is not None:
                new_edges[at, :] = new
            block = to >> (part.bit_length() - 1)
            none = jnp.zeros_like(new)
            spread = jnp.concatenate(
                [
                    jnp.where(block == b, new.astype(F32), 0.0).astype(BF16)
                    for b in range(BLOCKS)
                ],
                axis=1,
            )
            lists = [recv[pl.ds(t * rows + i, 1), :] & (part - 1) for i in range(rows)]
            acc[...] += dot(hot_columns(lists, part), spread)

        def body(t, carry):
            edge_tile(t, False)
            return carry

        lax.fori_loop(0, tiles - 1, body, 0)
        wait_rims(layer)
        edge_tile(tiles - 1, True)

        for b in range(BLOCKS):
            own = nodes[b * part : (b + 1) * part, :]
            got = acc[:, b * LANES : (b + 1) * LANES].astype(BF16)
            change = run_mlp([own, got], pair_w[layer], out_w, vec, 2 * layer + 1)
            new_nodes[b * part : (b + 1) * part, :] = (own.astype(F32) + change).astype(BF16)

    fine_layer(0, node, edge, e1, h1)

    width = slots.shape[0]
    lists = [pslot[i : i + 1, :] for i in range(nf // LANES)]
    slots[...] = dot(hot_columns(lists, width), h1[...]).astype(BF16).astype(F32)
    all_to_all(slots, arrived, pool_sem)
    lists = [pnode[0:1, i : i + LANES] for i in range(0, width, LANES)]
    pooled = normed(dot(hot_columns(lists, NC), arrived[...].astype(BF16))).astype(BF16)
    count = csend.shape[0]
    first = dot(hot_rows(columns(csend, 0, count), NC), pooled).astype(BF16)
    second = dot(hot_rows(columns(crecv, 0, count), NC), pooled).astype(BF16)
    coarse = run_mlp([first, second], pair_w[2], out_w, vec, 4).astype(BF16)
    lists = [crecv[i : i + 1, :] for i in range(count)]
    got = dot(hot_columns(lists, NC), coarse).astype(BF16)
    change = run_mlp([pooled, got], pair_w[3], out_w, vec, 5)
    coarse = (pooled.astype(F32) + change).astype(BF16)
    cols = [column(ipick[0:1, i : i + LANES]) for i in range(0, width, LANES)]
    picks[...] = dot(hot_rows(jnp.concatenate(cols, axis=0), NC), coarse)
    all_to_all(picks, back, back_sem)

    table = back[...].astype(BF16)
    table = jnp.concatenate([table, table], axis=0)
    which = lax.broadcasted_iota(jnp.int32, (width, LANES), 0)
    for i in range(0, nf, LANES):
        mix = jnp.zeros((width, LANES), F32)
        for j in range(3):
            mix += jnp.where(which == islot[j : j + 1, i : i + LANES], iwt[j : j + 1, i : i + LANES], 0.0)
        mix = mix.T
        high = mix.astype(BF16)
        low = (mix - high.astype(F32)).astype(BF16)
        mixed = dot(jnp.concatenate([high, low], axis=1), table)
        h2[i : i + LANES, :] = (h1[i : i + LANES, :].astype(F32) + mixed).astype(BF16)

    fine_layer(1, h2, e1, None, out)


def per_device(
    node_feat,
    edge_feat,
    edge_send,
    edge_recv,
    halo_send,
    pool_slot,
    pool_node,
    coarse_send,
    coarse_recv,
    interp_pick,
    interp_slot,
    interp_wt,
    edge_in_w,
    pair_in_w,
    out_w,
    mlp_vec,
):
    nf, width = node_feat.shape
    ef = edge_feat.shape[0]
    slots = pool_node.shape[1]
    peers = slots // SLOT
    vmem = pl.BlockSpec(memory_space=pltpu.VMEM)
    return pl.pallas_call(
        kernel,
        out_shape=jax.ShapeDtypeStruct((nf, width), BF16),
        in_specs=[vmem] * 16,
        out_specs=vmem,
        scratch_shapes=[
            pltpu.VMEM((ef, LANES), jnp.int32),
            pltpu.VMEM((ef, LANES), jnp.int32),
            pltpu.VMEM((ef, width), BF16),
            pltpu.VMEM((nf, width), BF16),
            pltpu.VMEM((nf, width), BF16),
            pltpu.VMEM((nf // BLOCKS, BLOCKS * width), F32),
            pltpu.VMEM((2, 2, RIM, width), BF16),
            pltpu.VMEM((2, 2, RIM, width), BF16),
            pltpu.VMEM((slots, width), F32),
            pltpu.VMEM((slots, width), F32),
            pltpu.VMEM((slots, width), F32),
            pltpu.VMEM((slots, width), F32),
            pltpu.SemaphoreType.DMA((2, 2, 2)),
            pltpu.SemaphoreType.DMA((2, peers)),
            pltpu.SemaphoreType.DMA((2, peers)),
        ],
        compiler_params=pltpu.CompilerParams(
            collective_id=0, has_side_effects=True, vmem_limit_bytes=56 * 1024 * 1024
        ),
    )(
        node_feat,
        edge_feat,
        edge_send.reshape(-1, LANES),
        edge_recv.reshape(-1, LANES),
        halo_send,
        pool_slot.reshape(-1, LANES),
        pool_node,
        coarse_send.reshape(-1, LANES),
        coarse_recv.reshape(-1, LANES),
        interp_pick,
        interp_slot,
        interp_wt,
        edge_in_w,
        pair_in_w,
        out_w,
        mlp_vec,
    )


def solution(mesh):
    rows = ("groups", "px", "py")
    placed = (
        P(rows, None),
        P(rows, None),
        P(rows),
        P(rows),
        P(rows, None),
        P(rows),
        P(rows, None),
        P(rows),
        P(rows),
        P(rows, None),
        P(None, rows),
        P(None, rows),
        P(),
        P(),
        P(),
        P(),
    )
    return jax.shard_map(
        per_device,
        mesh=mesh,
        in_specs=placed,
        out_specs=P(rows, None),
        check_vma=False,
    )
```

time: 290 us -> 55.4 us (0.19)
  local copies, waits for them, and re-layouts: 120 us -> 1.87 us
  other arithmetic: 105 us -> 0 us
  Pallas kernels: 0 us -> 53.3 us
  matrix products: 29.8 us -> 0 us
  starting transfers between devices: 19.5 us -> 0 us
  waiting for transfers between devices: 13.2 us -> 0 us
    gather x10 -> x0, local copies, waits for them, and re-layouts: 105 us -> none  [the longest x2 44.1 us: edge_step(): target = jnp.take(with_zero(nodes), receivers, axis=0)]
    scatter-add x5 -> x0, other arithmetic: 86.7 us -> none  [summed(): jax.ops.segment_sum(values.astype(jnp.float32), index, num_segments=count...]
    pallas_call x0 -> x1, Pallas kernels: none -> 53.3 us  [per_device(): pl.pallas_call(kernel, out_shape=jax.ShapeDtypeStruct((nf, width), BF16),...]
    dot_general x14 -> x0, matrix products: 29.8 us -> none  [the longest x8 18 us: run_mlp(): jnp.dot(piece, weight_in[place * width:(place + 1) * width], preferred_el...]
    all_to_all x2 -> x0, waiting for transfers between devices: 13.2 us -> none  [the longest x1 6.6 us: send_pooled(): lax.all_to_all(blocks, ('px', 'py'), split_axis=0, concat_axis=0, tiled=T...]
    all_to_all x2 -> x0, starting transfers between devices: 12.7 us -> none  [the longest x1 9.21 us: send_pooled(): lax.all_to_all(blocks, ('px', 'py'), split_axis=0, concat_axis=0, tiled=T...]
    convert_element_type x9 -> x0, other arithmetic: 8.88 us -> none  [the longest x2 2.44 us: summed(): values.astype(jnp.float32)]
    convert_element_type x3 -> x0, local copies, waits for them, and re-layouts: 6.78 us -> none  [summed(): values.astype(jnp.float32)]
  transfers between devices with their start and end apart: 6 -> 0, of which waited for: 2 -> 0; matrix products, arithmetic and copies ran while one was open for 19% -> 0% of each run, Pallas kernels for 0% -> 0%
where the time goes in v1:
time: 55.4 us; the launch traced here: 55.2 us
  Pallas kernels  53.3 us (96%)
  local copies, waits for them, and re-layouts  1.87 us (3%)
    pallas_call x1, Pallas kernels, per_device(): pl.pallas_call(kernel, out_shape=jax.ShapeDtypeStruct((nf, width), BF16),...  53.3 us
    unnamed x1, local copies, waits for them, and re-layouts  1.87 us

profile of v1, /device:TPU:0, one launch (start us, length us, event | category | flops | bytes accessed | tf_op | source)
XLA Modules:
  0.0 55.2 jit_solution(16131898321001961702)
XLA Ops:
  0.0 53.3 %shard_map.154 = bf16[2048,128]{1,0:T(8,128)(2,1)} custom-call(bf16[2048,128]{1,0:T(8,128)(2,1)} %node.1, bf16[6144,128]{1,0:T(8,128)(2,1)} %edge.1, s32[48,128]{1,0:T(8,128)} %bitcast.5, s32[48,128]{1,0:T(8,128)} %bitcast.6, s32[2,128]{1,0:T(2,128)} %halo.1, s32[16,128]{1,0:T(8,128)} %bitcast.7, s32[1,128]{1,0:T(1,128)} %pnode.1, s32[6,128]{1,0:T(8,128)} %bitcast.8, ...), custom_call_target="tpu_custom_call" | custom-call | tf_op jit(solution)/shard_map/pallas_call | solution.py:331
  53.3 1.9 %copy.18 = bf16[2048,128]{1,0:T(8,128)(2,1)} copy(bf16[2048,128]{1,0:T(8,128)(2,1)} %shard_map.154) | data formatting | bytes 1048576

commit v2 on v1

--- a/solution.py
+++ b/solution.py
@@ -12,7 +12,7 @@
 SLOT = 8
 RIM = 128
 BLOCKS = 4
-TILE = 1024
+TILE = 2048
 BF16 = jnp.bfloat16
 F32 = jnp.float32
 
@@ -103,6 +103,10 @@
     arrived,
     picks,
     back,
+    c_of,
+    c_to,
+    c_sum,
+    mixes,
     rim_sem,
     pool_sem,
     back_sem,
@@ -144,7 +148,8 @@
             device_id_type=pl.DeviceIdType.MESH,
         )
 
-    def send_rims(layer, table):
+    def send_rims(layer, nodes):
+        table = table_of(nodes)
         for side in range(2):
             rim_out[layer, side] = pick_rows(table, column(halo[side : side + 1, :]))
         if layer == 0:
@@ -199,7 +204,7 @@
             device_id_type=pl.DeviceIdType.MESH,
         )
 
-    def all_to_all(src, dst, sem):
+    def all_to_all(src, dst, sem, meanwhile):
         def start(d, carry):
             exchange(src, dst, sem, d).start()
             return carry
@@ -212,11 +217,13 @@
         lax.fori_loop(1, peers, start, 0)
         mine = pl.ds(pl.multiple_of(me * SLOT, SLOT), SLOT)
         dst[mine, :] = src[mine, :]
+        result = meanwhile()
         lax.fori_loop(1, peers, finish, 0)
+        return result
 
     def fine_layer(layer, nodes, edges, new_edges, new_nodes):
-        table = table_of(nodes)
-        send_rims(layer, table)
+        if layer:
+            send_rims(layer, nodes)
         acc[...] = jnp.zeros(acc.shape, F32)
 
         def edge_tile(t, last):
@@ -230,13 +237,13 @@
                 to = rcol[at, :]
                 of = scol[at, :]
             tab = table_of(nodes)
-            source = pick_rows(tab, of - RIM)
+            source = pick_rows(tab, (of[: TILE - eb] if last else of) - RIM)
             if last:
                 tail = of[TILE - eb :]
                 rim_row = jnp.where(tail < RIM, tail, tail - nf)
                 rim = jnp.concatenate([rims[layer, 0], rims[layer, 1]], axis=0)
                 more = dot(hot_rows(rim_row, eb), rim).astype(BF16)
-                source = jnp.concatenate([source[: TILE - eb], more], axis=0)
+                source = jnp.concatenate([source, more], axis=0)
             target = pick_rows(tab, to)
             old = edges[at, :]
             change = run_mlp([source, target, old], edge_w[layer], out_w, vec, 2 * layer)
@@ -244,7 +251,6 @@
             if new_edges is not None:
                 new_edges[at, :] = new
             block = to >> (part.bit_length() - 1)
-            none = jnp.zeros_like(new)
             spread = jnp.concatenate(
                 [
                     jnp.where(block == b, new.astype(F32), 0.0).astype(BF16)
@@ -256,6 +262,8 @@
             acc[...] += dot(hot_columns(lists, part), spread)
 
         def body(t, carry):
+            if layer == 0:
+                pl.when(t == (tiles - 1) // 2)(lambda: send_rims(layer, nodes))
             edge_tile(t, False)
             return carry
 
@@ -274,33 +282,41 @@
     width = slots.shape[0]
     lists = [pslot[i : i + 1, :] for i in range(nf // LANES)]
     slots[...] = dot(hot_columns(lists, width), h1[...]).astype(BF16).astype(F32)
-    all_to_all(slots, arrived, pool_sem)
+    count = csend.shape[0]
+
+    def coarse_lists():
+        c_of[...] = hot_rows(columns(csend, 0, count), NC)
+        c_to[...] = hot_rows(columns(crecv, 0, count), NC)
+        c_sum[...] = hot_columns([crecv[i : i + 1, :] for i in range(count)], NC)
+
+    all_to_all(slots, arrived, pool_sem, coarse_lists)
     lists = [pnode[0:1, i : i + LANES] for i in range(0, width, LANES)]
     pooled = normed(dot(hot_columns(lists, NC), arrived[...].astype(BF16))).astype(BF16)
-    count = csend.shape[0]
-    first = dot(hot_rows(columns(csend, 0, count), NC), pooled).astype(BF16)
-    second = dot(hot_rows(columns(crecv, 0, count), NC), pooled).astype(BF16)
+    first = dot(c_of[...], pooled).astype(BF16)
+    second = dot(c_to[...], pooled).astype(BF16)
     coarse = run_mlp([first, second], pair_w[2], out_w, vec, 4).astype(BF16)
-    lists = [crecv[i : i + 1, :] for i in range(count)]
-    got = dot(hot_columns(lists, NC), coarse).astype(BF16)
+    got = dot(c_sum[...], coarse).astype(BF16)
     change = run_mlp([pooled, got], pair_w[3], out_w, vec, 5)
     coarse = (pooled.astype(F32) + change).astype(BF16)
     cols = [column(ipick[0:1, i : i + LANES]) for i in range(0, width, LANES)]
     picks[...] = dot(hot_rows(jnp.concatenate(cols, axis=0), NC), coarse)
-    all_to_all(picks, back, back_sem)
-
+    which = lax.broadcasted_iota(jnp.int32, (width, LANES), 0)
+
+    def parent_weights():
+        for i in range(0, nf, LANES):
+            mix = jnp.zeros((width, LANES), F32)
+            for j in range(3):
+                parent = islot[j : j + 1, i : i + LANES]
+                mix += jnp.where(which == parent, iwt[j : j + 1, i : i + LANES], 0.0)
+            mix = mix.T
+            high = mix.astype(BF16)
+            low = (mix - high.astype(F32)).astype(BF16)
+            mixes[i : i + LANES, :] = jnp.concatenate([high, low], axis=1)
+
+    all_to_all(picks, back, back_sem, parent_weights)
     table = back[...].astype(BF16)
-    table = jnp.concatenate([table, table], axis=0)
-    which = lax.broadcasted_iota(jnp.int32, (width, LANES), 0)
-    for i in range(0, nf, LANES):
-        mix = jnp.zeros((width, LANES), F32)
-        for j in range(3):
-            mix += jnp.where(which == islot[j : j + 1, i : i + LANES], iwt[j : j + 1, i : i + LANES], 0.0)
-        mix = mix.T
-        high = mix.astype(BF16)
-        low = (mix - high.astype(F32)).astype(BF16)
-        mixed = dot(jnp.concatenate([high, low], axis=1), table)
-        h2[i : i + LANES, :] = (h1[i : i + LANES, :].astype(F32) + mixed).astype(BF16)
+    mixed = dot(mixes[...], jnp.concatenate([table, table], axis=0))
+    h2[...] = (h1[...].astype(F32) + mixed).astype(BF16)
 
     fine_layer(1, h2, e1, None, out)
 
@@ -346,6 +362,10 @@
             pltpu.VMEM((slots, width), F32),
             pltpu.VMEM((slots, width), F32),
             pltpu.VMEM((slots, width), F32),
+            pltpu.VMEM((coarse_send.shape[0], NC), BF16),
+            pltpu.VMEM((coarse_send.shape[0], NC), BF16),
+            pltpu.VMEM((NC, coarse_send.shape[0]), BF16),
+            pltpu.VMEM((nf, 2 * slots), BF16),
             pltpu.SemaphoreType.DMA((2, 2, 2)),
             pltpu.SemaphoreType.DMA((2, peers)),
             pltpu.SemaphoreType.DMA((2, peers)),

time: 55.4 us -> 49.3 us (0.89)
  Pallas kernels: 53.3 us -> 47.2 us
    pallas_call x1, Pallas kernels: 53.3 us -> 47.2 us  [per_device(): pl.pallas_call(kernel, out_shape=jax.ShapeDtypeStruct((nf, width), BF16),...]
where the time goes in v2:
time: 49.3 us; the launch traced here: 49.1 us
  Pallas kernels  47.2 us (96%)
  local copies, waits for them, and re-layouts  1.87 us (4%)
    pallas_call x1, Pallas kernels, per_device(): pl.pallas_call(kernel, out_shape=jax.ShapeDtypeStruct((nf, width), BF16),...  47.2 us
    unnamed x1, local copies, waits for them, and re-layouts  1.87 us

profile of v2, /device:TPU:0, one launch (start us, length us, event | category | flops | bytes accessed | tf_op | source)
XLA Modules:
  0.0 49.1 jit_solution(8225214205317080524)
XLA Ops:
  0.0 47.2 %shard_map.154 = bf16[2048,128]{1,0:T(8,128)(2,1)} custom-call(bf16[2048,128]{1,0:T(8,128)(2,1)} %node.1, bf16[6144,128]{1,0:T(8,128)(2,1)} %edge.1, s32[48,128]{1,0:T(8,128)} %bitcast.5, s32[48,128]{1,0:T(8,128)} %bitcast.6, s32[2,128]{1,0:T(2,128)} %halo.1, s32[16,128]{1,0:T(8,128)} %bitcast.7, s32[1,128]{1,0:T(1,128)} %pnode.1, s32[6,128]{1,0:T(8,128)} %bitcast.8, ...), custom_call_target="tpu_custom_call" | custom-call | tf_op jit(solution)/shard_map/pallas_call | solution.py:347
  47.2 1.9 %copy.18 = bf16[2048,128]{1,0:T(8,128)(2,1)} copy(bf16[2048,128]{1,0:T(8,128)(2,1)} %shard_map.154) | data formatting | bytes 1048576
